TPU v7x, 32 devices: a whole 2x2x4 slice. The times are simulated.
32 devices in a mesh: tok: 8 (over z, y), head: 4 (over x, core).
Axes of the slice: x: 2, y: 2, z: 4, core: 2. Of those that a mesh axis runs over, the one named last changes fastest.
Arguments:
- hidden_in: bfloat16 [4096, 2048], P(('tok', 'head')), may hold values from -6 to 6
- context_len: int32 [8], P('tok'), may hold values from 1 to 2048, 8192 in all
- page_table: int32 [8, 16], P('tok'), may hold values from 0 to 15, as said below
- paged_cache: bfloat16 [2, 128, 128, 2048], P(None, 'tok', None, 'head'), may hold values from -139 to 139
- attn_gain: bfloat16 [2048], replicated, may hold values from 0.5 to 1.5
- proj_weight: bfloat16 [3, 2048, 2048], P(None, None, 'head'), may hold values from -0.125 to 0.125
- proj_bias: bfloat16 [3, 2048], P(None, 'head'), may hold values from -3 to 3
- out_weight: bfloat16 [2048, 2048], P('head'), may hold values from -0.125 to 0.125
- mlp_gain: bfloat16 [2048], replicated, may hold values from 0.5 to 1.5
- expert_ids: int32 [4096, 4], P(('tok', 'head')), may hold values from 0 to 15, all different within a row; in each aligned block of 128 rows (0 to 127, 128 to 255, ...) at most 40 rows name the same one
- route_weight: float32 [4096, 4], P(('tok', 'head')), may hold values from 0.05 to 0.5
- w_experts_in: bfloat16 [32, 2048, 1408], P(('tok', 'head')), may hold values from -0.125 to 0.125
- w_experts_out: bfloat16 [32, 704, 2048], P(('tok', 'head')), may hold values from -0.15625 to 0.15625
- w_shared_in: bfloat16 [2048, 2, 5632], P(None, None, 'head'), may hold values from -0.125 to 0.125
- w_shared_out: bfloat16 [5632, 2048], P('head'), may hold values from -0.078125 to 0.078125
- shared_gate: bfloat16 [2048], replicated, may hold values from -0.125 to 0.125
Outputs:
- layer_out: bfloat16 [4096, 2048], P(('tok', 'head'))
Inputs may be any that keep to these rules, and one draw needn't show every extreme that they name: `page_table`: each row is a permutation of the pool's pages. `context_len`: some request has exactly 2048 cached tokens. `expert_ids`: the experts of a row differ; within the 128 rows of one device no expert is named more than 40 times, a bound that some block reaches.
All inputs are finite; a program needn't handle non-finite values. No bound on the sum of `context_len` on one device may be relied on, other than what follows from the above.
Results may differ from a plain program's by a relative error of at most 0.02.
Values may be sent and summed in bfloat16 or wider, within the bound.
A program may use at most 128 MiB of HBM per device.

v0:
```python
import math

import jax
import jax.numpy as jnp
from jax import lax
from jax.experimental import pallas as pl
from jax.experimental.pallas import tpu as pltpu
from jax.sharding import PartitionSpec as P

HD = 128
BLOCK = 256
DEEP = (((1,), (1,)), ((), ()))
DOWN = (((0,), (0,)), ((), ()))


EPS = 1e-06
THETA = 1000000.0


def rms_scale(values, gain):
    wide = values.astype(jnp.float32)
    spread = jnp.mean(wide * wide, axis=-1, keepdims=True)
    return (wide * lax.rsqrt(spread + EPS) * gain.astype(jnp.float32)).astype(jnp.bfloat16)


def attend_kernel(
    table, context_len, rows, gain, weight, bias, cosines, sines, cache, out_weight, out, q_all, k_all, v_all
):
    stretch, width = rows.shape
    lanes = weight.shape[2]
    heads = lanes // HD
    pages, page = cache.shape[1], cache.shape[2]
    span = pages * page
    context = context_len[0]

    @pl.loop(0, pages)
    def _(index):
        place = table[0, index]
        at = pl.ds(pl.multiple_of(index * page, page), page)
        k_all[at, :] = cache[0, place]
        v_all[at, :] = cache[1, place]

    @pl.loop(0, stretch // BLOCK)
    def _(block):
        start = pl.multiple_of(block * BLOCK, BLOCK)
        at = pl.ds(start, BLOCK)
        new_at = pl.ds(pl.multiple_of(span + start, BLOCK), BLOCK)
        wide = rows[at, :].astype(jnp.float32)
        spread = jnp.mean(wide * wide, axis=-1, keepdims=True)
        normed = (wide * lax.rsqrt(spread + EPS) * gain[...]).astype(jnp.bfloat16)
        cos, sin = cosines[at, :], sines[at, :]
        for part, kept, place in ((0, q_all, at), (1, k_all, new_at), (2, v_all, new_at)):
            value = jnp.dot(normed, weight[part], preferred_element_type=jnp.float32) + bias[part]
            if part < 2:
                turned = []
                for head in range(heads):
                    one = value[:, head * HD : (head + 1) * HD]
                    turned.append(one * cos + pltpu.roll(one, HD // 2, 1) * sin)
                value = jnp.concatenate(turned, axis=1)
            kept[place, :] = value.astype(jnp.bfloat16)

    factor = math.log2(math.e) / math.sqrt(HD)

    @pl.loop(0, stretch // BLOCK)
    def _(block):
        start = pl.multiple_of(block * BLOCK, BLOCK)
        at = pl.ds(start, BLOCK)
        old_ok = lax.broadcasted_iota(jnp.int32, (BLOCK, span), 1) < context
        new_ok = lax.broadcasted_iota(jnp.int32, (BLOCK, stretch), 1) <= (
            lax.broadcasted_iota(jnp.int32, (BLOCK, stretch), 0) + start
        )
        found = []
        for head in range(heads):
            cols = slice(head * HD, (head + 1) * HD)
            query = q_all[at, cols]
            old = lax.dot_general(query, k_all[:span, cols], DEEP, preferred_element_type=jnp.float32)
            new = lax.dot_general(query, k_all[span:, cols], DEEP, preferred_element_type=jnp.float32)
            old = jnp.where(old_ok, old, -1e30)
            new = jnp.where(new_ok, new, -1e30)
            largest = jnp.maximum(
                jnp.max(old, axis=-1, keepdims=True), jnp.max(new, axis=-1, keepdims=True)
            )
            old = jnp.exp2((old - largest) * factor)
            new = jnp.exp2((new - largest) * factor)
            total = jnp.sum(old, axis=-1, keepdims=True) + jnp.sum(new, axis=-1, keepdims=True)
            value = jnp.dot(
                old.astype(jnp.bfloat16), v_all[:span, cols], preferred_element_type=jnp.float32
            ) + jnp.dot(
                new.astype(jnp.bfloat16), v_all[span:, cols], preferred_element_type=jnp.float32
            )
            found.append((value / total).astype(jnp.bfloat16))
        out[at, :] = jnp.dot(
            jnp.concatenate(found, axis=1), out_weight[...], preferred_element_type=jnp.float32
        ).astype(jnp.bfloat16)


def attend(gathered, context_len, page_table, cache, gain, weight, bias, out_weight):
    stretch, width = gathered.shape
    lanes = weight.shape[2]
    span = cache.shape[1] * cache.shape[2]
    frequency = THETA ** (-(jnp.arange(HD // 2, dtype=jnp.float32) * 2.0 / HD))
    positions = context_len[0] + jnp.arange(stretch, dtype=jnp.int32)
    angles = positions.astype(jnp.float32)[:, None] * frequency[None, :]
    cosines = jnp.tile(jnp.cos(angles), (1, 2))
    sines = jnp.sin(angles)
    sines = jnp.concatenate([-sines, sines], axis=1)
    smem = pl.BlockSpec(memory_space=pltpu.SMEM)
    vmem = pl.BlockSpec(memory_space=pltpu.VMEM)
    return pl.pallas_call(
        attend_kernel,
        out_shape=jax.ShapeDtypeStruct((stretch, width), jnp.bfloat16),
        in_specs=[smem, smem] + [vmem] * 8,
        out_specs=vmem,
        scratch_shapes=[
            pltpu.VMEM((stretch, lanes), jnp.bfloat16),
            pltpu.VMEM((span + stretch, lanes), jnp.bfloat16),
            pltpu.VMEM((span + stretch, lanes), jnp.bfloat16),
        ],
        compiler_params=pltpu.CompilerParams(vmem_limit_bytes=52 * 1024 * 1024),
        cost_estimate=pl.CostEstimate(
            flops=12 * 10**9, bytes_accessed=20 * 10**6, transcendentals=5 * 10**6
        ),
    )(
        page_table,
        context_len,
        gathered,
        gain.astype(jnp.float32)[None],
        weight,
        bias.astype(jnp.float32)[:, None, :],
        cosines,
        sines,
        cache,
        out_weight,
    )


def per_device(
    hidden_in,
    context_len,
    page_table,
    paged_cache,
    attn_gain,
    proj_weight,
    proj_bias,
    out_weight,
    mlp_gain,
    expert_ids,
    route_weight,
    w_experts_in,
    w_experts_out,
    w_shared_in,
    w_shared_out,
    shared_gate,
):
    tok_rows, width = hidden_in.shape
    half = width // 2
    head_lanes = lax.axis_size("head")
    device_count = lax.axis_size("tok") * head_lanes
    expert_count = device_count // 2
    top_count = expert_ids.shape[1]
    capacity = 2 * max(1, tok_rows * top_count * 5 // (8 * expert_count))
    slots = expert_count * capacity
    core = lax.axis_index("head") % 2
    swap = [(lane, lane ^ 1) for lane in range(head_lanes)]

    named = expert_ids[:, :, None] == jnp.arange(expert_count, dtype=jnp.int32)
    chosen = jnp.any(named, axis=1)
    share = jnp.sum(jnp.where(named, route_weight[:, :, None], 0.0), axis=1)
    row_ids = jnp.arange(tok_rows, dtype=jnp.int32)
    below = (row_ids[:, None] > row_ids[None, :]).astype(jnp.bfloat16)
    earlier = jnp.dot(below, chosen.astype(jnp.bfloat16), preferred_element_type=jnp.float32)
    spot = jnp.where(chosen, earlier.astype(jnp.int32), -1)
    taken = spot.T[:, None, :] == jnp.arange(capacity, dtype=jnp.int32)[None, :, None]
    dispatch = taken.astype(jnp.bfloat16).reshape(slots, tok_rows)
    combine = jnp.where(taken, share.T[:, None, :], 0.0).reshape(slots, tok_rows)
    combine_high = combine.astype(jnp.bfloat16)
    combine_low = (combine - combine_high.astype(jnp.float32)).astype(jnp.bfloat16)

    gathered = lax.all_gather(hidden_in, "head", axis=0, tiled=True)
    attn_part = attend(
        gathered, context_len, page_table, paged_cache, attn_gain, proj_weight, proj_bias, out_weight
    )
    attn_own = lax.psum_scatter(attn_part, "head", scatter_dimension=0, tiled=True)
    resid = (hidden_in.astype(jnp.float32) + attn_own.astype(jnp.float32)).astype(jnp.bfloat16)
    mixed = rms_scale(resid, mlp_gain)

    buffer = [
        jnp.dot(dispatch, mixed[:, at : at + half], preferred_element_type=jnp.float32)
        .astype(jnp.bfloat16)
        .reshape(expert_count, capacity, half)
        for at in (0, half)
    ]
    sending = jnp.stack(buffer, axis=1).reshape(device_count, capacity, half)
    arrived = lax.all_to_all(sending, ("tok", "head"), split_axis=0, concat_axis=0, tiled=True)

    mixed_all = lax.all_gather(mixed, "head", axis=0, tiled=True)
    inner = jnp.einsum("td,dcf->tcf", mixed_all, w_shared_in, preferred_element_type=jnp.float32)
    activated = (jax.nn.silu(inner[:, 0]) * inner[:, 1]).astype(jnp.bfloat16)
    shared_part = jnp.dot(activated, w_shared_out, preferred_element_type=jnp.float32).astype(
        jnp.bfloat16
    )
    arrived, shared_part = lax.optimization_barrier((arrived, shared_part))
    shared_own = lax.psum_scatter(
        shared_part, "head", scatter_dimension=0, tiled=True
    ).astype(jnp.float32)
    gate = jax.nn.sigmoid(jnp.dot(mixed, shared_gate, preferred_element_type=jnp.float32))

    own = arrived.reshape(device_count * capacity, half)
    other = lax.ppermute(own, "head", swap)
    tokens = jnp.concatenate(
        [jnp.where(core == 0, own, other), jnp.where(core == 0, other, own)], axis=1
    )
    inner = jnp.dot(tokens, w_experts_in[0], preferred_element_type=jnp.float32)
    middle = inner.shape[1] // 2
    activated = (jax.nn.silu(inner[:, :middle]) * inner[:, middle:]).astype(jnp.bfloat16)
    finished = jnp.dot(activated, w_experts_out[0], preferred_element_type=jnp.float32).astype(
        jnp.bfloat16
    )
    low, high = finished[:, :half], finished[:, half:]
    partner = lax.ppermute(jnp.where(core == 0, high, low), "head", swap)
    merged = (
        jnp.where(core == 0, low, high).astype(jnp.float32) + partner.astype(jnp.float32)
    ).astype(jnp.bfloat16)
    returned = lax.all_to_all(
        merged.reshape(device_count, capacity, half),
        ("tok", "head"),
        split_axis=0,
        concat_axis=0,
        tiled=True,
    ).reshape(expert_count, 2, capacity, half)
    routed = []
    for side in range(2):
        part = returned[:, side].reshape(slots, half)
        routed.append(
            lax.dot_general(combine_high, part, DOWN, preferred_element_type=jnp.float32)
            + lax.dot_general(combine_low, part, DOWN, preferred_element_type=jnp.float32)
        )
    routed = jnp.concatenate(routed, axis=1)
    return (resid.astype(jnp.float32) + gate[:, None] * shared_own + routed).astype(jnp.bfloat16)


def solution(mesh):
    in_specs = (
        P(("tok", "head"), None),
        P("tok"),
        P("tok", None),
        P(None, "tok", None, "head"),
        P(),
        P(None, None, "head"),
        P(None, "head"),
        P("head", None),
        P(),
        P(("tok", "head"), None),
        P(("tok", "head"), None),
        P(("tok", "head"), None, None),
        P(("tok", "head"), None, None),
        P(None, None, "head"),
        P("head", None),
        P(),
    )
    out_specs = P(("tok", "head"), None)
    return jax.shard_map(
        per_device, mesh=mesh, in_specs=in_specs, out_specs=out_specs, check_vma=False
    )
```

profile of v0, /device:TPU:0, one launch (start us, length us, event | category | flops | bytes accessed | tf_op | source)
XLA Modules:
  0.0 271.7 jit_solution(8257396147609638236)
XLA Ops:
  6.5 0.0 copy-start
  6.5 0.0 all-gather.3.cloned.1.call-start
  6.5 0.7 all-gather.3.cloned.1.call-update
  7.3 0.0 reduce-scatter.3.cloned.1.call-start
  8.1 0.7 reshape.193.bias
  8.8 0.7 broadcast_in_dim.60
  9.5 1.8 fusion.29
  11.3 0.8 copy.33
  12.1 0.9 tile.4
  13.0 0.1 copy.34.cosines
  13.1 1.2 pad_maximum_fusion.1.sines
  14.3 20.0 %all-gather.3.cloned.1.call-done.rows = bf16[512,2048]{1,0:T(8,128)(2,1)} async-done(((bf16[128,2048]{1,0:T(8,128)(2,1)}), bf16[512,2048]{1,0:T(8,128)(2,1)}) %all-gather.3.cloned.1.call-update) | async-done | bytes 2097168 | tf_op jit(solution)/shard_map/all_gather | solution.py:179
  34.2 0.0 copy-done.1
  34.2 21.1 %shard_map.154 = bf16[512,2048]{1,0:T(8,128)(2,1)} custom-call(s32[1,16]{1,0:T(1,128)S(1)} %copy-done.1, s32[1]{0:T(128)} %copy.43.context_len, bf16[512,2048]{1,0:T(8,128)(2,1)} %all-gather.3.cloned.1.call-done.rows, f32[1,2048]{1,0:T(1,128)S(1)} %bitcast.70, bf16[3,2048,512]{2,1,0:T(8,128)(2,1)} %weight.1, f32[3,1,512]{2,1,0:T(1,128)S(1)} %reshape.193.bias, ...), custom_call_target="tpu_custom_call" | custom-call | flops 12000000000 | bytes 20000000 | tf_op jit(solution)/shard_map/pallas_call | solution.py:109
  55.4 0.0 reduce-scatter.3.cloned.1.call-update
  55.4 0.0 all-gather.5.cloned.1.call-start
  55.4 0.0 copy-done.8
  55.5 0.1 eq.74
  55.6 0.0 copy-done.7
  55.6 0.1 fusion.16
  55.7 0.2 bitcast_compare_fusion
  55.9 31.1 %reduce-scatter.3.cloned.1.call-done = bf16[128,2048]{1,0:T(8,128)(2,1)} async-done(((bf16[512,2048]{1,0:T(8,128)(2,1)}), bf16[128,2048]{1,0:T(8,128)(2,1)}) %reduce-scatter.3.cloned.1.call-update) | async-done | bytes 524304 | tf_op jit(solution)/shard_map/reduce_scatter | solution.py:183
  87.0 1.5 fusion.21
  88.5 0.0 copy-done.3
  88.5 2.0 fusion.23
  90.6 0.0 all-gather.5.cloned.1.call-update
  90.6 1.4 convolution_convert_fusion.2
  92.0 1.4 convolution_convert_fusion.3
  93.5 1.7 pad_maximum_fusion
  95.2 4.9 %all-to-all-start = ((bf16[32,40,1024]{2,1,0:T(8,128)(2,1)}), bf16[32,40,1024]{2,1,0:T(8,128)(2,1)}, u32[]{:S(2)}, u32[]{:S(2)}) async-start(bf16[32,40,1024]{2,1,0:T(8,128)(2,1)} %bitcast.75), calls=%async_computation.1 | async-start | bytes 5242880 | tf_op jit(solution)/shard_map/all_to_all | solution.py:194
  100.1 36.4 %all-gather.5.cloned.1.call-done = bf16[512,2048]{1,0:T(8,128)(2,1)} async-done(((bf16[128,2048]{1,0:T(8,128)(2,1)}), bf16[512,2048]{1,0:T(8,128)(2,1)}) %all-gather.5.cloned.1.call-update) | async-done | bytes 2097168 | tf_op jit(solution)/shard_map/all_gather | solution.py:196
  136.6 11.2 %fusion = f32[512,2,1408]{2,0,1:T(8,128)S(1)} fusion(bf16[2048,2,1408]{2,1,0:T(2,128)(2,1)} %param.29, bf16[512,2048]{1,0:T(8,128)(2,1)} %all-gather.5.cloned.1.call-done), kind=kOutput, calls=%fused_computation | convolution fusion | flops 5905580032 | bytes 19398656 | tf_op jit(solution)/shard_map/td,dcf->tcf/dot_general | solution.py:197
  147.8 7.3 %convolution_convert_fusion.1 = bf16[512,2048]{1,0:T(8,128)(2,1)} fusion(bf16[1408,2048]{1,0:T(8,128)(2,1)} %param.30, f32[512,2,1408]{2,0,1:T(8,128)S(1)} %fusion), kind=kOutput, calls=%fused_computation.11 | convolution fusion | flops 2958163968 | bytes 13631488 | tf_op jit(solution)/shard_map/dot_general | solution.py:199
  155.1 5.2 %all-to-all-done = bf16[32,40,1024]{2,1,0:T(8,128)(2,1)} async-done(((bf16[32,40,1024]{2,1,0:T(8,128)(2,1)}), bf16[32,40,1024]{2,1,0:T(8,128)(2,1)}, u32[]{:S(2)}, u32[]{:S(2)}) %all-to-all-start) | async-done | bytes 2621472 | tf_op jit(solution)/shard_map/all_to_all | solution.py:194
  160.3 0.0 collective-permute-start
  160.3 5.2 %collective-permute-done = bf16[1280,1024]{1,0:T(8,128)(2,1)} collective-permute-done((bf16[1280,1024]{1,0:T(8,128)(2,1)}, bf16[1280,1024]{1,0:T(8,128)(2,1)}, u32[]{:S(2)}, u32[]{:S(2)}) %collective-permute-start) | collective-permute-done | bytes 2621472 | tf_op jit(solution)/shard_map/ppermute | solution.py:209
  165.5 2.9 %broadcast_select_fusion.2 = (bf16[1280,1024]{1,0:T(8,128)(2,1)S(1)}, bf16[1280,1024]{1,0:T(8,128)(2,1)S(1)}) fusion(bf16[1280,1024]{1,0:T(8,128)(2,1)} %collective-permute-done, pred[]{:T(512)S(6)} %eq.79, bf16[32,40,1024]{2,1,0:T(8,128)(2,1)} %all-to-all-done), kind=kLoop, calls=%fused_computation.20 | loop fusion | flops 2621440 | bytes 10485761 | tf_op jit(solution)/shard_map/jit(_where)/select_n | solution.py:211
  168.4 11.1 %fusion.2 = f32[1280,1408]{1,0:T(8,128)S(1)} fusion(bf16[1,2048,1408]{2,1,0:T(8,128)(2,1)} %param.27, bf16[1280,1024]{1,0:T(8,128)(2,1)S(1)} %get-tuple-element.10, bf16[1280,1024]{1,0:T(8,128)(2,1)S(1)} %get-tuple-element.9), kind=kOutput, calls=%fused_computation.3 | convolution fusion | flops 7392460800 | bytes 18219008 | tf_op jit(solution)/shard_map/dot_general | solution.py:213
  179.5 0.0 copy-done
  179.5 4.9 %convolution_convert_fusion = bf16[1280,2048]{1,0:T(8,128)(2,1)S(1)} fusion(bf16[1,704,2048]{2,1,0:T(8,128)(2,1)S(1)} %copy-done, f32[1280,1408]{1,0:T(8,128)S(1)} %fusion.2), kind=kOutput, calls=%fused_computation.2 | convolution fusion | flops 3699015680 | bytes 15990784 | tf_op jit(solution)/shard_map/dot_general | solution.py:216
  184.4 0.3 broadcast_select_fusion
  184.7 0.2 collective-permute-start.1
  184.8 4.8 %collective-permute-done.1 = bf16[1280,1024]{1,0:T(8,128)(2,1)S(1)} collective-permute-done((bf16[1280,1024]{1,0:T(8,128)(2,1)S(1)}, bf16[1280,1024]{1,0:T(8,128)(2,1)S(1)}, u32[]{:S(2)}, u32[]{:S(2)}) %collective-permute-start.1) | collective-permute-done | bytes 2621472 | tf_op jit(solution)/shard_map/ppermute | solution.py:220
  189.6 3.4 %add_convert_fusion = bf16[1280,1024]{1,0:T(8,128)(2,1)} fusion(bf16[1280,1024]{1,0:T(8,128)(2,1)S(1)} %collective-permute-done.1, pred[]{:T(512)S(6)} %eq.79, bf16[1280,2048]{1,0:T(8,128)(2,1)S(1)} %convolution_convert_fusion), kind=kLoop, calls=%fused_computation.8 | loop fusion | flops 6553600 | bytes 10485761 | tf_op jit(solution)/shard_map/convert_element_type | solution.py:223
  193.1 4.0 %all-to-all-start.1 = ((bf16[32,40,1024]{2,1,0:T(8,128)(2,1)}), bf16[32,40,1024]{2,1,0:T(8,128)(2,1)}, u32[]{:S(2)}, u32[]{:S(2)}) async-start(bf16[32,40,1024]{2,1,0:T(8,128)(2,1)} %bitcast.76), calls=%async_computation.3 | async-start | bytes 5242880 | tf_op jit(solution)/shard_map/all_to_all | solution.py:224
  197.0 0.0 reduce-scatter.5.cloned.1.call-start
  197.1 0.5 reduce-scatter.5.cloned.1.call-update
  197.6 0.0 copy-done.9
  197.6 0.0 copy-done.10
  197.7 0.7 fusion.26
  198.4 0.7 select_convert_fusion
  199.1 0.0 copy-done.2
  199.1 0.2 fusion.20
  199.3 57.9 %all-to-all-done.1 = bf16[32,40,1024]{2,1,0:T(8,128)(2,1)} async-done(((bf16[32,40,1024]{2,1,0:T(8,128)(2,1)}), bf16[32,40,1024]{2,1,0:T(8,128)(2,1)}, u32[]{:S(2)}, u32[]{:S(2)}) %all-to-all-start.1) | async-done | bytes 2621472 | tf_op jit(solution)/shard_map/all_to_all | solution.py:224
  257.2 2.0 fusion.34
  259.2 0.0 copy-start.5
  259.2 0.4 fusion.36
  259.6 0.4 fusion.35
  260.0 0.0 copy-start.4
  260.1 0.1 copy-done.5
  260.1 1.2 convolution_add_fusion
  261.3 1.2 convolution_add_fusion.1
  262.5 0.0 copy-done.4
  262.5 2.6 fusion.25
  (18 shorter events, 0.1 us)
Async XLA Ops:
  6.5 172.9 %copy-start = (bf16[1,704,2048]{2,1,0:T(8,128)(2,1)S(1)}, bf16[1,704,2048]{2,1,0:T(8,128)(2,1)}, u32[]{:S(2)}) copy-start(bf16[1,704,2048]{2,1,0:T(8,128)(2,1)} %param.28) | copy-start | bytes 8650756
  6.5 27.7 %copy-start.1 = (s32[1,16]{1,0:T(1,128)S(1)}, s32[1,16]{1,0:T(1,128)}, u32[]{:S(2)}) copy-start(s32[1,16]{1,0:T(1,128)} %table.1) | copy-start | bytes 196
  6.5 27.7 %all-gather.3.cloned.1.call-start = ((), (), s32[]{:S(2)}) async-start(), calls=%async_computation.4 | async-start | bytes 2621440 | tf_op jit(solution)/shard_map/all_gather | solution.py:179
  7.3 79.8 %reduce-scatter.3.cloned.1.call-start = ((), (), s32[]{:S(2)}) async-start(), calls=%async_computation.5 | async-start | bytes 2621440 | tf_op jit(solution)/shard_map/reduce_scatter | solution.py:183
  34.2 21.2 %copy-start.8 = (bf16[2048]{0:T(1024)(128)(2,1)S(1)}, bf16[2048]{0:T(1024)(128)(2,1)}, u32[]{:S(2)}) copy-start(bf16[2048]{0:T(1024)(128)(2,1)} %param.24) | copy-start | bytes 12292
  34.2 21.3 %copy-start.7 = (s32[128,4]{0,1:T(4,128)S(1)}, s32[128,4]{0,1:T(4,128)}, u32[]{:S(2)}) copy-start(s32[128,4]{0,1:T(4,128)} %param.25) | copy-start | bytes 6148
  55.4 33.2 %copy-start.3 = (bf16[128,2048]{1,0:T(8,128)(2,1)S(1)}, bf16[128,2048]{1,0:T(8,128)(2,1)}, u32[]{:S(2)}) copy-start(bf16[128,2048]{1,0:T(8,128)(2,1)} %param.16) | copy-start | bytes 1572868
  55.4 81.2 %all-gather.5.cloned.1.call-start = ((), (), s32[]{:S(2)}) async-start(), calls=%async_computation.6 | async-start | bytes 2621440 | tf_op jit(solution)/shard_map/all_gather | solution.py:196
  95.2 65.0 %all-to-all-start = ((bf16[32,40,1024]{2,1,0:T(8,128)(2,1)}), bf16[32,40,1024]{2,1,0:T(8,128)(2,1)}, u32[]{:S(2)}, u32[]{:S(2)}) async-start(bf16[32,40,1024]{2,1,0:T(8,128)(2,1)} %bitcast.75), calls=%async_computation.1 | async-start | bytes 5242880 | tf_op jit(solution)/shard_map/all_to_all | solution.py:194
  160.3 5.3 %collective-permute-start = (bf16[1280,1024]{1,0:T(8,128)(2,1)}, bf16[1280,1024]{1,0:T(8,128)(2,1)}, u32[]{:S(2)}, u32[]{:S(2)}) collective-permute-start(bf16[1280,1024]{1,0:T(8,128)(2,1)} %bitcast.16), channel_id=1, source_target_pairs={{0,1},{1,0},{2,3},{3,2},{4,5},{5,4},{6,7},{7,6},{8,9},{9,8},{10,11... | collective-permute-start | bytes 7864328 | tf_op jit(solution)/shard_map/ppermute | solution.py:209
  184.7 5.0 %collective-permute-start.1 = (bf16[1280,1024]{1,0:T(8,128)(2,1)S(1)}, bf16[1280,1024]{1,0:T(8,128)(2,1)S(1)}, u32[]{:S(2)}, u32[]{:S(2)}) collective-permute-start(bf16[1280,1024]{1,0:T(8,128)(2,1)S(1)} %broadcast_select_fusion), channel_id=1, source_target_pairs={{0,1},{1,0},{2,3},{3,2},{4,5},{5,4},{6,7},{7,6},{8,9},{9,8},{10,11... | collective-permute-start | bytes 7864328 | tf_op jit(solution)/shard_map/ppermute | solution.py:220
  193.1 4.6 %copy-start.9 = (bf16[2048]{0:T(1024)(128)(2,1)S(1)}, bf16[2048]{0:T(1024)(128)(2,1)}, u32[]{:S(2)}) copy-start(bf16[2048]{0:T(1024)(128)(2,1)} %param.31) | copy-start | bytes 12292
  193.1 4.6 %copy-start.10 = (f32[128,4]{0,1:T(4,128)S(1)}, f32[128,4]{0,1:T(4,128)}, u32[]{:S(2)}) copy-start(f32[128,4]{0,1:T(4,128)} %param.26) | copy-start | bytes 6148
  193.1 6.0 %copy-start.2 = (bf16[128,2048]{1,0:T(8,128)(2,1)S(1)}, bf16[128,2048]{1,0:T(8,128)(2,1)}, u32[]{:S(2)}) copy-start(bf16[128,2048]{1,0:T(8,128)(2,1)} %fusion.23) | copy-start | bytes 1572868
  193.1 64.1 %all-to-all-start.1 = ((bf16[32,40,1024]{2,1,0:T(8,128)(2,1)}), bf16[32,40,1024]{2,1,0:T(8,128)(2,1)}, u32[]{:S(2)}, u32[]{:S(2)}) async-start(bf16[32,40,1024]{2,1,0:T(8,128)(2,1)} %bitcast.76), calls=%async_computation.3 | async-start | bytes 5242880 | tf_op jit(solution)/shard_map/all_to_all | solution.py:224
  197.0 65.5 %reduce-scatter.5.cloned.1.call-start = ((), (), s32[]{:S(2)}) async-start(), calls=%async_computation.7 | async-start | bytes 2621440 | tf_op jit(solution)/shard_map/reduce_scatter | solution.py:203
  257.2 2.0 copy-start.6
  259.2 0.9 copy-start.5
  260.0 2.5 copy-start.4
Sparse Core Ops, SparseCore 0:
  8.9 25.2 all-gather.2
  55.5 31.4 reduce-scatter.2
  90.7 45.8 all-gather.4
  200.2 40.4 reduce-scatter.4
where the time goes:
time: 272 us
  waiting for transfers between devices  162 us (60%)
  matrix products  40.9 us (15%)
  Pallas kernels  21.1 us (8%)
  other arithmetic  19.7 us (7%)
  between operations  14.1 us (5%)
  starting transfers between devices  9.19 us (3%)
  local copies, waits for them, and re-layouts  4.7 us (2%)
    all_to_all x1, waiting for transfers between devices, per_device(): lax.all_to_all(merged.reshape(device_count, capacity, half), ('tok', 'hea...  57.9 us
    all_gather x1, waiting for transfers between devices, per_device(): mixed_all = lax.all_gather(mixed, 'head', axis=0, tiled=True)  36.4 us
    reduce_scatter x1, waiting for transfers between devices, per_device(): lax.psum_scatter(attn_part, 'head', scatter_dimension=0, tiled=True)  31.1 us
    pallas_call x1, Pallas kernels, attend(): pl.pallas_call(attend_kernel, out_shape=jax.ShapeDtypeStruct((stretch, wi...  21.1 us
    all_gather x1, waiting for transfers between devices, per_device(): gathered = lax.all_gather(hidden_in, 'head', axis=0, tiled=True)  20 us
    dot_general x1, matrix products, per_device(): jnp.einsum('td,dcf->tcf', mixed_all, w_shared_in, preferred_element_type=...  11.2 us
    dot_general x1, matrix products, per_device(): inner = jnp.dot(tokens, w_experts_in[0], preferred_element_type=jnp.float32)  11.1 us
    dot_general x1, matrix products, per_device(): jnp.dot(activated, w_shared_out, preferred_element_type=jnp.float32)  7.33 us
  transfers between devices with their start and end apart: 8, of which 7 were waited for; matrix products, arithmetic and copies ran while one was open for 13% of the time, Pallas kernels for 0%

commit v1 on v0

--- a/solution.py
+++ b/solution.py
@@ -24,7 +24,7 @@
 
 
 def attend_kernel(
-    table, context_len, rows, gain, weight, bias, cosines, sines, cache, out_weight, out, q_all, k_all, v_all
+    table, context_len, rows, gain, weight, bias, query_pos, key_pos, cosines, sines, cache, out_weight, out, q_all, k_all, v_all
 ):
     stretch, width = rows.shape
     lanes = weight.shape[2]
@@ -66,9 +66,7 @@
         start = pl.multiple_of(block * BLOCK, BLOCK)
         at = pl.ds(start, BLOCK)
         old_ok = lax.broadcasted_iota(jnp.int32, (BLOCK, span), 1) < context
-        new_ok = lax.broadcasted_iota(jnp.int32, (BLOCK, stretch), 1) <= (
-            lax.broadcasted_iota(jnp.int32, (BLOCK, stretch), 0) + start
-        )
+        new_ok = key_pos[...] <= query_pos[at, :]
         found = []
         for head in range(heads):
             cols = slice(head * HD, (head + 1) * HD)
@@ -94,12 +92,41 @@
         ).astype(jnp.bfloat16)
 
 
-def attend(gathered, context_len, page_table, cache, gain, weight, bias, out_weight):
+def lane_swap(values, bit, lanes):
+    return lax.ppermute(values, "head", [(lane, lane ^ bit) for lane in range(lanes)])
+
+
+def lane_order(lanes):
+    order, bit = [0], lanes // 2
+    while bit:
+        order, bit = order + [step ^ bit for step in order], bit // 2
+    return order
+
+
+def gather_lanes(values, lanes):
+    bit = lanes // 2
+    while bit:
+        values = jnp.concatenate([values, lane_swap(values, bit, lanes)], axis=0)
+        bit //= 2
+    return values
+
+
+def sum_lanes(values, lanes):
+    total, bit = values, 1
+    while bit < lanes:
+        kept = total.shape[0] // 2
+        arrived = lane_swap(total[kept:].astype(jnp.bfloat16), bit, lanes)
+        total = total[:kept].astype(jnp.float32) + arrived.astype(jnp.float32)
+        bit *= 2
+    return total
+
+
+def attend(gathered, order, context_len, page_table, cache, gain, weight, bias, out_weight):
     stretch, width = gathered.shape
     lanes = weight.shape[2]
     span = cache.shape[1] * cache.shape[2]
     frequency = THETA ** (-(jnp.arange(HD // 2, dtype=jnp.float32) * 2.0 / HD))
-    positions = context_len[0] + jnp.arange(stretch, dtype=jnp.int32)
+    positions = context_len[0] + order
     angles = positions.astype(jnp.float32)[:, None] * frequency[None, :]
     cosines = jnp.tile(jnp.cos(angles), (1, 2))
     sines = jnp.sin(angles)
@@ -109,7 +136,7 @@
     return pl.pallas_call(
         attend_kernel,
         out_shape=jax.ShapeDtypeStruct((stretch, width), jnp.bfloat16),
-        in_specs=[smem, smem] + [vmem] * 8,
+        in_specs=[smem, smem] + [vmem] * 10,
         out_specs=vmem,
         scratch_shapes=[
             pltpu.VMEM((stretch, lanes), jnp.bfloat16),
@@ -127,6 +154,8 @@
         gain.astype(jnp.float32)[None],
         weight,
         bias.astype(jnp.float32)[:, None, :],
+        order[:, None],
+        order[None, :],
         cosines,
         sines,
         cache,
@@ -176,12 +205,14 @@
     combine_high = combine.astype(jnp.bfloat16)
     combine_low = (combine - combine_high.astype(jnp.float32)).astype(jnp.bfloat16)
 
-    gathered = lax.all_gather(hidden_in, "head", axis=0, tiled=True)
+    gathered = gather_lanes(hidden_in, head_lanes)
+    owners = jnp.array(lane_order(head_lanes), jnp.int32) ^ lax.axis_index("head")
+    order = (owners[:, None] * tok_rows + row_ids[None, :]).reshape(-1)
     attn_part = attend(
-        gathered, context_len, page_table, paged_cache, attn_gain, proj_weight, proj_bias, out_weight
-    )
-    attn_own = lax.psum_scatter(attn_part, "head", scatter_dimension=0, tiled=True)
-    resid = (hidden_in.astype(jnp.float32) + attn_own.astype(jnp.float32)).astype(jnp.bfloat16)
+        gathered, order, context_len, page_table, paged_cache, attn_gain, proj_weight, proj_bias, out_weight
+    )
+    attn_own = sum_lanes(attn_part, head_lanes)
+    resid = (hidden_in.astype(jnp.float32) + attn_own).astype(jnp.bfloat16)
     mixed = rms_scale(resid, mlp_gain)
 
     buffer = [
@@ -193,16 +224,14 @@
     sending = jnp.stack(buffer, axis=1).reshape(device_count, capacity, half)
     arrived = lax.all_to_all(sending, ("tok", "head"), split_axis=0, concat_axis=0, tiled=True)
 
-    mixed_all = lax.all_gather(mixed, "head", axis=0, tiled=True)
+    mixed_all = gather_lanes(mixed, head_lanes)
     inner = jnp.einsum("td,dcf->tcf", mixed_all, w_shared_in, preferred_element_type=jnp.float32)
     activated = (jax.nn.silu(inner[:, 0]) * inner[:, 1]).astype(jnp.bfloat16)
     shared_part = jnp.dot(activated, w_shared_out, preferred_element_type=jnp.float32).astype(
         jnp.bfloat16
     )
     arrived, shared_part = lax.optimization_barrier((arrived, shared_part))
-    shared_own = lax.psum_scatter(
-        shared_part, "head", scatter_dimension=0, tiled=True
-    ).astype(jnp.float32)
+    shared_own = sum_lanes(shared_part, head_lanes)
     gate = jax.nn.sigmoid(jnp.dot(mixed, shared_gate, preferred_element_type=jnp.float32))
 
     own = arrived.reshape(device_count * capacity, half)

time: 272 us -> 245 us (0.901)
  waiting for transfers between devices: 162 us -> 133 us
  between operations: 14.1 us -> 1.12 us
  starting transfers between devices: 9.19 us -> 19.6 us
  matrix products: 40.9 us -> 34.2 us
  local copies, waits for them, and re-layouts: 4.7 us -> 11.3 us
  other arithmetic: 19.7 us -> 23.8 us
    ppermute x0 -> x8, waiting for transfers between devices: none -> 66.9 us  [lane_swap(): lax.ppermute(values, 'head', [(lane, lane ^ bit) for lane in range(lanes)])]
    all_gather x2 -> x0, waiting for transfers between devices: 56.4 us -> none  [the longest x1 36.4 us: per_device(): mixed_all = lax.all_gather(mixed, 'head', axis=0, tiled=True)]
    reduce_scatter x2 -> x0, waiting for transfers between devices: 31.1 us -> none  [the longest x1 31.1 us: per_device(): lax.psum_scatter(attn_part, 'head', scatter_dimension=0, tiled=True)]
    ppermute x0 -> x8, starting transfers between devices: none -> 9.04 us  [lane_swap(): lax.ppermute(values, 'head', [(lane, lane ^ bit) for lane in range(lanes)])]
    all_to_all x1, waiting for transfers between devices: 57.9 us -> 52.5 us  [per_device(): lax.all_to_all(merged.reshape(device_count, capacity, half), ('tok', 'hea...]
    concatenate x0 -> x3, other arithmetic: none -> 5.34 us  [gather_lanes(): values = jnp.concatenate([values, lane_swap(values, bit, lanes)], axis=0)]
    unnamed x23 -> x43, local copies, waits for them, and re-layouts: 0.12 us -> 4.96 us
    slice x0 -> x4, local copies, waits for them, and re-layouts: none -> 3.79 us  [sum_lanes(): arrived = lane_swap(total[kept:].astype(jnp.bfloat16), bit, lanes)]
  transfers between devices with their start and end apart: 8 -> 12, of which waited for: 7 -> 10; matrix products, arithmetic and copies ran while one was open for 13% -> 11% of each run, Pallas kernels for 0% -> 0%
where the time goes in v1:
time: 245 us; the launch traced here: 244 us
  waiting for transfers between devices  133 us (54%)
  matrix products  34.2 us (14%)
  other arithmetic  23.8 us (10%)
  Pallas kernels  21 us (9%)
  starting transfers between devices  19.6 us (8%)
  local copies, waits for them, and re-layouts  11.3 us (5%)
    ppermute x8, waiting for transfers between devices, lane_swap(): lax.ppermute(values, 'head', [(lane, lane ^ bit) for lane in range(lanes)])  66.9 us
    all_to_all x1, waiting for transfers between devices, per_device(): lax.all_to_all(merged.reshape(device_count, capacity, half), ('tok', 'hea...  52.5 us
    pallas_call x1, Pallas kernels, attend(): pl.pallas_call(attend_kernel, out_shape=jax.ShapeDtypeStruct((stretch, wi...  21 us
    dot_general x1, matrix products, per_device(): inner = jnp.dot(tokens, w_experts_in[0], preferred_element_type=jnp.float32)  11.1 us
    dot_general x1, matrix products, per_device(): jnp.einsum('td,dcf->tcf', mixed_all, w_shared_in, preferred_element_type=...  10.6 us
    ppermute x8, starting transfers between devices, lane_swap(): lax.ppermute(values, 'head', [(lane, lane ^ bit) for lane in range(lanes)])  9.04 us
    all_to_all x1, starting transfers between devices, per_device(): lax.all_to_all(sending, ('tok', 'head'), split_axis=0, concat_axis=0, til...  6.39 us
    concatenate x3, other arithmetic, gather_lanes(): values = jnp.concatenate([values, lane_swap(values, bit, lanes)], axis=0)  5.34 us
  transfers between devices with their start and end apart: 12, of which 10 were waited for; matrix products, arithmetic and copies ran while one was open for 11% of the time, Pallas kernels for 0%

profile of v1, /device:TPU:0, one launch (start us, length us, event | category | flops | bytes accessed | tf_op | source)
XLA Modules:
  0.0 244.1 jit_solution(743073284394637951)
XLA Ops:
  0.0 3.0 %collective-permute-start = (bf16[128,2048]{1,0:T(8,128)(2,1)}, bf16[128,2048]{1,0:T(8,128)(2,1)S(1)}, u32[]{:S(2)}, u32[]{:S(2)}) collective-permute-start(bf16[128,2048]{1,0:T(8,128)(2,1)} %param.17), channel_id=1, source_target_pairs={{0,2},{1,3},{2,0},{3,1},{4,6},{5,7},{6,4},{7,5},{8,10},{9,11},{10,... | collective-permute-start | bytes 1572872 | tf_op jit(solution)/shard_map/ppermute | solution.py:96
  3.0 12.1 %collective-permute-done = bf16[128,2048]{1,0:T(8,128)(2,1)S(1)} collective-permute-done((bf16[128,2048]{1,0:T(8,128)(2,1)}, bf16[128,2048]{1,0:T(8,128)(2,1)S(1)}, u32[]{:S(2)}, u32[]{:S(2)}) %collective-permute-start) | collective-permute-done | bytes 524320 | tf_op jit(solution)/shard_map/ppermute | solution.py:96
  15.2 0.8 copy-done.10
  15.9 2.1 pad_maximum_fusion.2
  18.7 0.7 xor_multiply_fusion
  19.5 1.8 fusion.35
  21.3 0.1 copy.36
  21.4 0.1 copy.38.cosines
  21.6 0.1 copy.37.query_pos
  21.8 1.2 pad_maximum_fusion.4.sines
  23.0 3.1 %pad_maximum_fusion.1.rows = bf16[512,2048]{1,0:T(8,128)(2,1)} fusion(bf16[256,2048]{1,0:T(8,128)(2,1)} %collective-permute-done.1, bf16[128,2048]{1,0:T(8,128)(2,1)} %copy-done.10, bf16[128,2048]{1,0:T(8,128)(2,1)} %param.17), kind=kLoop, calls=%fused_computation.21 | loop fusion | flops 6291456 | bytes 4194304 | tf_op jit(solution)/shard_map/concatenate | solution.py:109
  26.1 21.0 %shard_map.163 = bf16[512,2048]{1,0:T(8,128)(2,1)} custom-call(s32[1,16]{1,0:T(1,128)S(1)} %copy-done.1, s32[1]{0:T(128)} %copy.47.context_len, bf16[512,2048]{1,0:T(8,128)(2,1)} %pad_maximum_fusion.1.rows, f32[1,2048]{1,0:T(1,128)S(1)} %bitcast.76, bf16[3,2048,512]{2,1,0:T(8,128)(2,1)} %weight.1, f32[3,1,512]{2,1,0:T(1,128)S(1)} %reshape.249.bias, ...), custom_call_target="tpu_custom_call" | custom-call | flops 12000000000 | bytes 20000000 | tf_op jit(solution)/shard_map/pallas_call | solution.py:136
  47.1 1.4 slice.75
  48.6 0.6 collective-permute-start.2
  49.1 2.3 collective-permute-done.2
  51.4 0.4 convert_add_fusion.1
  51.8 1.4 copy-done.4
  53.2 0.9 slice.129
  54.0 1.8 collective-permute-start.3
  55.8 0.1 eq.74
  55.9 0.1 fusion.19
  56.1 0.2 bitcast_compare_fusion
  56.2 12.3 %collective-permute-done.3 = bf16[128,2048]{1,0:T(8,128)(2,1)} collective-permute-done((bf16[128,2048]{1,0:T(8,128)(2,1)}, bf16[128,2048]{1,0:T(8,128)(2,1)}, u32[]{:S(2)}, u32[]{:S(2)}) %collective-permute-start.3) | collective-permute-done | bytes 524320 | tf_op jit(solution)/shard_map/ppermute | solution.py:96
  68.6 1.7 fusion.24
  70.3 0.2 fusion.26
  70.5 0.6 copy-done.5
  71.1 0.5 convolution_convert_fusion.3
  71.6 0.5 convolution_convert_fusion.2
  72.1 1.8 pad_maximum_fusion
  73.8 6.4 %all-to-all-start = ((bf16[32,40,1024]{2,1,0:T(8,128)(2,1)}), bf16[32,40,1024]{2,1,0:T(8,128)(2,1)}, u32[]{:S(2)}, u32[]{:S(2)}) async-start(bf16[32,40,1024]{2,1,0:T(8,128)(2,1)} %bitcast.81), calls=%async_computation | async-start | bytes 5242880 | tf_op jit(solution)/shard_map/all_to_all | solution.py:225
  80.2 1.6 collective-permute-start.4
  81.8 36.8 %collective-permute-done.4 = bf16[128,2048]{1,0:T(8,128)(2,1)S(1)} collective-permute-done((bf16[128,2048]{1,0:T(8,128)(2,1)S(1)}, bf16[128,2048]{1,0:T(8,128)(2,1)S(1)}, u32[]{:S(2)}, u32[]{:S(2)}) %collective-permute-start.4) | collective-permute-done | bytes 524320 | tf_op jit(solution)/shard_map/ppermute | solution.py:96
  118.6 0.1 pad_maximum_fusion.3
  118.8 2.6 %collective-permute-done.5 = bf16[256,2048]{1,0:T(8,128)(2,1)S(1)} collective-permute-done((bf16[256,2048]{1,0:T(8,128)(2,1)S(1)}, bf16[256,2048]{1,0:T(8,128)(2,1)S(1)}, u32[]{:S(2)}, u32[]{:S(2)}) %collective-permute-start.5) | collective-permute-done | bytes 1048608 | tf_op jit(solution)/shard_map/ppermute | solution.py:96
  121.4 10.6 %fusion = f32[512,2,1408]{2,0,1:T(8,128)S(1)} fusion(bf16[2048,2,1408]{2,1,0:T(2,128)(2,1)} %param.30, bf16[256,2048]{1,0:T(8,128)(2,1)S(1)} %collective-permute-done.5, bf16[128,2048]{1,0:T(8,128)(2,1)S(1)} %collective-permute-done.4, bf16[128,2048]{1,0:T(8,128)(2,1)S(1)} %fusion.26), kind=kOutput, calls=%fused_computation | convolution fusion | flops 5911871488 | bytes 19398656 | tf_op jit(solution)/shard_map/td,dcf->tcf/dot_general | solution.py:228
  132.0 4.7 %convolution_convert_fusion.1 = bf16[512,2048]{1,0:T(8,128)(2,1)} fusion(bf16[1408,2048]{1,0:T(8,128)(2,1)S(1)} %bitcast.93, f32[512,2,1408]{2,0,1:T(8,128)S(1)} %fusion), kind=kOutput, calls=%fused_computation.11 | convolution fusion | flops 2958163968 | bytes 13631488 | tf_op jit(solution)/shard_map/dot_general | solution.py:230
  136.8 3.6 %all-to-all-done = bf16[32,40,1024]{2,1,0:T(8,128)(2,1)} async-done(((bf16[32,40,1024]{2,1,0:T(8,128)(2,1)}), bf16[32,40,1024]{2,1,0:T(8,128)(2,1)}, u32[]{:S(2)}, u32[]{:S(2)}) %all-to-all-start) | async-done | bytes 2621472 | tf_op jit(solution)/shard_map/all_to_all | solution.py:225
  140.4 5.2 %collective-permute-done.8 = bf16[1280,1024]{1,0:T(8,128)(2,1)} collective-permute-done((bf16[1280,1024]{1,0:T(8,128)(2,1)}, bf16[1280,1024]{1,0:T(8,128)(2,1)}, u32[]{:S(2)}, u32[]{:S(2)}) %collective-permute-start.8) | collective-permute-done | bytes 2621472 | tf_op jit(solution)/shard_map/ppermute | solution.py:238
  145.6 2.9 %broadcast_select_fusion.2 = (bf16[1280,1024]{1,0:T(8,128)(2,1)S(1)}, bf16[1280,1024]{1,0:T(8,128)(2,1)S(1)}) fusion(bf16[1280,1024]{1,0:T(8,128)(2,1)} %collective-permute-done.8, pred[]{:T(512)S(6)} %eq.79, bf16[32,40,1024]{2,1,0:T(8,128)(2,1)} %all-to-all-done), kind=kLoop, calls=%fused_computation.20 | loop fusion | flops 2621440 | bytes 10485761 | tf_op jit(solution)/shard_map/jit(_where)/select_n | solution.py:240
  148.5 11.1 %fusion.2 = f32[1280,1408]{1,0:T(8,128)S(1)} fusion(bf16[1,2048,1408]{2,1,0:T(8,128)(2,1)} %param.28, bf16[1280,1024]{1,0:T(8,128)(2,1)S(1)} %get-tuple-element.12, bf16[1280,1024]{1,0:T(8,128)(2,1)S(1)} %get-tuple-element.11), kind=kOutput, calls=%fused_computation.3 | convolution fusion | flops 7392460800 | bytes 18219008 | tf_op jit(solution)/shard_map/dot_general | solution.py:242
  159.6 4.9 %convolution_convert_fusion = bf16[1280,2048]{1,0:T(8,128)(2,1)S(1)} fusion(bf16[1,704,2048]{2,1,0:T(8,128)(2,1)S(1)} %copy-done, f32[1280,1408]{1,0:T(8,128)S(1)} %fusion.2), kind=kOutput, calls=%fused_computation.2 | convolution fusion | flops 3699015680 | bytes 15990784 | tf_op jit(solution)/shard_map/dot_general | solution.py:245
  164.5 0.3 broadcast_select_fusion
  164.8 0.2 collective-permute-start.9
  165.0 4.8 %collective-permute-done.9 = bf16[1280,1024]{1,0:T(8,128)(2,1)S(1)} collective-permute-done((bf16[1280,1024]{1,0:T(8,128)(2,1)S(1)}, bf16[1280,1024]{1,0:T(8,128)(2,1)S(1)}, u32[]{:S(2)}, u32[]{:S(2)}) %collective-permute-start.9) | collective-permute-done | bytes 2621472 | tf_op jit(solution)/shard_map/ppermute | solution.py:249
  169.7 3.5 %add_convert_fusion = bf16[1280,1024]{1,0:T(8,128)(2,1)} fusion(bf16[1280,1024]{1,0:T(8,128)(2,1)S(1)} %collective-permute-done.9, pred[]{:T(512)S(6)} %eq.79, bf16[1280,2048]{1,0:T(8,128)(2,1)S(1)} %convolution_convert_fusion), kind=kLoop, calls=%fused_computation.8 | loop fusion | flops 6553600 | bytes 10485761 | tf_op jit(solution)/shard_map/convert_element_type | solution.py:252
  173.2 3.9 %all-to-all-start.1 = ((bf16[32,40,1024]{2,1,0:T(8,128)(2,1)}), bf16[32,40,1024]{2,1,0:T(8,128)(2,1)}, u32[]{:S(2)}, u32[]{:S(2)}) async-start(bf16[32,40,1024]{2,1,0:T(8,128)(2,1)} %bitcast.82), calls=%async_computation.1 | async-start | bytes 5242880 | tf_op jit(solution)/shard_map/all_to_all | solution.py:253
  177.1 1.4 slice.65
  178.6 0.3 collective-permute-start.6
  178.9 0.7 select_convert_fusion
  179.6 0.7 fusion.32
  180.3 0.2 fusion.23
  180.5 0.8 collective-permute-done.6
  181.3 0.4 convert_add_fusion
  181.7 1.3 copy-done.2
  183.1 1.8 collective-permute-start.7
  184.9 52.5 %all-to-all-done.1 = bf16[32,40,1024]{2,1,0:T(8,128)(2,1)} async-done(((bf16[32,40,1024]{2,1,0:T(8,128)(2,1)}), bf16[32,40,1024]{2,1,0:T(8,128)(2,1)}, u32[]{:S(2)}, u32[]{:S(2)}) %all-to-all-start.1) | async-done | bytes 2621472 | tf_op jit(solution)/shard_map/all_to_all | solution.py:253
  237.4 2.0 fusion.42
  239.4 0.4 fusion.43
  239.8 0.4 convolution_add_fusion.1
  240.2 0.4 fusion.44
  240.7 0.4 convolution_add_fusion
  241.1 0.7 copy-done.3
  241.8 0.1 copy-done.6
  241.9 2.2 fusion.28
  (54 shorter events, 0.4 us)
Async XLA Ops:
  0.0 159.6 %copy-start = (bf16[1,704,2048]{2,1,0:T(8,128)(2,1)S(1)}, bf16[1,704,2048]{2,1,0:T(8,128)(2,1)}, u32[]{:S(2)}) copy-start(bf16[1,704,2048]{2,1,0:T(8,128)(2,1)} %param.29) | copy-start | bytes 8650756
  0.0 21.7 %copy-start.14 = (bf16[2048]{0:T(1024)(128)(2,1)S(1)}, bf16[2048]{0:T(1024)(128)(2,1)}, u32[]{:S(2)}) copy-start(bf16[2048]{0:T(1024)(128)(2,1)} %param.21) | copy-start | bytes 12292
  0.0 21.7 %copy-start.17 = (bf16[3,512]{1,0:T(4,128)(2,1)S(1)}, bf16[3,512]{1,0:T(4,128)(2,1)}, u32[]{:S(2)}) copy-start(bf16[3,512]{1,0:T(4,128)(2,1)} %param.23) | copy-start | bytes 9220
  0.0 15.1 %collective-permute-start = (bf16[128,2048]{1,0:T(8,128)(2,1)}, bf16[128,2048]{1,0:T(8,128)(2,1)S(1)}, u32[]{:S(2)}, u32[]{:S(2)}) collective-permute-start(bf16[128,2048]{1,0:T(8,128)(2,1)} %param.17), channel_id=1, source_target_pairs={{0,2},{1,3},{2,0},{3,1},{4,6},{5,7},{6,4},{7,5},{8,10},{9,11},{10,... | collective-permute-start | bytes 1572872 | tf_op jit(solution)/shard_map/ppermute | solution.py:96
  15.2 0.8 copy-start.10
  18.1 4.9 %collective-permute-start.1 = (bf16[256,2048]{1,0:T(8,128)(2,1)}, bf16[256,2048]{1,0:T(8,128)(2,1)}, u32[]{:S(2)}, u32[]{:S(2)}) collective-permute-start(bf16[256,2048]{1,0:T(8,128)(2,1)} %pad_maximum_fusion.2), channel_id=1, source_target_pairs={{0,1},{1,0},{2,3},{3,2},{4,5},{5,4},{6,7},{7,6},{8,9},{9,8},{10,11... | collective-permute-start | bytes 3145736 | tf_op jit(solution)/shard_map/ppermute | solution.py:96
  21.6 4.5 %copy-start.1 = (s32[1,16]{1,0:T(1,128)S(1)}, s32[1,16]{1,0:T(1,128)}, u32[]{:S(2)}) copy-start(s32[1,16]{1,0:T(1,128)} %table.1) | copy-start | bytes 196
  47.1 4.3 %copy-start.9 = (bf16[512,2048]{1,0:T(8,128)(2,1)S(1)}, bf16[512,2048]{1,0:T(8,128)(2,1)}, u32[]{:S(2)}) copy-start(bf16[512,2048]{1,0:T(8,128)(2,1)} %shard_map.163) | copy-start | bytes 6291460
  48.5 7.3 %copy-start.15 = (bf16[2048]{0:T(1024)(128)(2,1)S(1)}, bf16[2048]{0:T(1024)(128)(2,1)}, u32[]{:S(2)}) copy-start(bf16[2048]{0:T(1024)(128)(2,1)} %param.25) | copy-start | bytes 12292
  48.6 7.3 %copy-start.13 = (s32[128,4]{0,1:T(4,128)S(1)}, s32[128,4]{0,1:T(4,128)}, u32[]{:S(2)}) copy-start(s32[128,4]{0,1:T(4,128)} %param.26) | copy-start | bytes 6148
  48.6 20.0 %copy-start.7 = (bf16[128,2048]{1,0:T(8,128)(2,1)S(1)}, bf16[128,2048]{1,0:T(8,128)(2,1)}, u32[]{:S(2)}) copy-start(bf16[128,2048]{1,0:T(8,128)(2,1)} %param.17) | copy-start | bytes 1572868
  48.6 2.9 %collective-permute-start.2 = (bf16[256,2048]{1,0:T(8,128)(2,1)S(1)}, bf16[256,2048]{1,0:T(8,128)(2,1)S(1)}, u32[]{:S(2)}, u32[]{:S(2)}) collective-permute-start(bf16[256,2048]{1,0:T(8,128)(2,1)S(1)} %slice.75), channel_id=1, source_target_pairs={{0,1},{1,0},{2,3},{3,2},{4,5},{5,4},{6,7},{7,6},{8,9},{9,8},{10,11... | collective-permute-start | bytes 3145736 | tf_op jit(solution)/shard_map/ppermute | solution.py:96
  51.8 1.4 copy-start.4
  54.0 14.5 %collective-permute-start.3 = (bf16[128,2048]{1,0:T(8,128)(2,1)}, bf16[128,2048]{1,0:T(8,128)(2,1)}, u32[]{:S(2)}, u32[]{:S(2)}) collective-permute-start(bf16[128,2048]{1,0:T(8,128)(2,1)} %slice.129), channel_id=1, source_target_pairs={{0,2},{1,3},{2,0},{3,1},{4,6},{5,7},{6,4},{7,5},{8,10},{9,11},{10,... | collective-permute-start | bytes 1572872 | tf_op jit(solution)/shard_map/ppermute | solution.py:96
  70.3 0.8 copy-start.5
  73.8 66.6 %all-to-all-start = ((bf16[32,40,1024]{2,1,0:T(8,128)(2,1)}), bf16[32,40,1024]{2,1,0:T(8,128)(2,1)}, u32[]{:S(2)}, u32[]{:S(2)}) async-start(bf16[32,40,1024]{2,1,0:T(8,128)(2,1)} %bitcast.81), calls=%async_computation | async-start | bytes 5242880 | tf_op jit(solution)/shard_map/all_to_all | solution.py:225
  80.2 38.4 %collective-permute-start.4 = (bf16[128,2048]{1,0:T(8,128)(2,1)S(1)}, bf16[128,2048]{1,0:T(8,128)(2,1)S(1)}, u32[]{:S(2)}, u32[]{:S(2)}) collective-permute-start(bf16[128,2048]{1,0:T(8,128)(2,1)S(1)} %fusion.26), channel_id=1, source_target_pairs={{0,2},{1,3},{2,0},{3,1},{4,6},{5,7},{6,4},{7,5},{8,10},{9,11},{10,... | collective-permute-start | bytes 1572872 | tf_op jit(solution)/shard_map/ppermute | solution.py:96
  118.6 13.4 %slice-start = ((s8[5767168]{0:T(1024)(128)(4,1)}), s8[4194304]{0:T(1024)(128)(4,1)S(1)}, s32[]{:S(2)}) async-start(s8[5767168]{0:T(1024)(128)(4,1)} %bitcast.92), calls=%async_computation.2 | async-start | bytes 8388608
  118.7 13.3 %slice-start.1 = ((s8[5767168]{0:T(1024)(128)(4,1)}), s8[1572864]{0:T(1024)(128)(4,1)S(1)}, s32[]{:S(2)}) async-start(s8[5767168]{0:T(1024)(128)(4,1)} %bitcast.92), calls=%async_computation.3 | async-start | bytes 3145728
  118.7 2.7 %collective-permute-start.5 = (bf16[256,2048]{1,0:T(8,128)(2,1)S(1)}, bf16[256,2048]{1,0:T(8,128)(2,1)S(1)}, u32[]{:S(2)}, u32[]{:S(2)}) collective-permute-start(bf16[256,2048]{1,0:T(8,128)(2,1)S(1)} %pad_maximum_fusion.3), channel_id=1, source_target_pairs={{0,1},{1,0},{2,3},{3,2},{4,5},{5,4},{6,7},{7,6},{8,9},{9,8},{10,11... | collective-permute-start | bytes 3145736 | tf_op jit(solution)/shard_map/ppermute | solution.py:96
  140.4 5.3 %collective-permute-start.8 = (bf16[1280,1024]{1,0:T(8,128)(2,1)}, bf16[1280,1024]{1,0:T(8,128)(2,1)}, u32[]{:S(2)}, u32[]{:S(2)}) collective-permute-start(bf16[1280,1024]{1,0:T(8,128)(2,1)} %bitcast.19), channel_id=1, source_target_pairs={{0,1},{1,0},{2,3},{3,2},{4,5},{5,4},{6,7},{7,6},{8,9},{9,8},{10,11... | collective-permute-start | bytes 7864328 | tf_op jit(solution)/shard_map/ppermute | solution.py:238
  164.8 5.0 %collective-permute-start.9 = (bf16[1280,1024]{1,0:T(8,128)(2,1)S(1)}, bf16[1280,1024]{1,0:T(8,128)(2,1)S(1)}, u32[]{:S(2)}, u32[]{:S(2)}) collective-permute-start(bf16[1280,1024]{1,0:T(8,128)(2,1)S(1)} %broadcast_select_fusion), channel_id=1, source_target_pairs={{0,1},{1,0},{2,3},{3,2},{4,5},{5,4},{6,7},{7,6},{8,9},{9,8},{10,11... | collective-permute-start | bytes 7864328 | tf_op jit(solution)/shard_map/ppermute | solution.py:249
  173.2 5.6 %copy-start.16 = (bf16[2048]{0:T(1024)(128)(2,1)S(1)}, bf16[2048]{0:T(1024)(128)(2,1)}, u32[]{:S(2)}) copy-start(bf16[2048]{0:T(1024)(128)(2,1)} %param.32) | copy-start | bytes 12292
  173.2 5.7 %copy-start.18 = (f32[128,4]{0,1:T(4,128)S(1)}, f32[128,4]{0,1:T(4,128)}, u32[]{:S(2)}) copy-start(f32[128,4]{0,1:T(4,128)} %param.27) | copy-start | bytes 6148
  173.2 64.2 %all-to-all-start.1 = ((bf16[32,40,1024]{2,1,0:T(8,128)(2,1)}), bf16[32,40,1024]{2,1,0:T(8,128)(2,1)}, u32[]{:S(2)}, u32[]{:S(2)}) async-start(bf16[32,40,1024]{2,1,0:T(8,128)(2,1)} %bitcast.82), calls=%async_computation.1 | async-start | bytes 5242880 | tf_op jit(solution)/shard_map/all_to_all | solution.py:253
  177.1 4.2 %copy-start.8 = (bf16[512,2048]{1,0:T(8,128)(2,1)S(1)}, bf16[512,2048]{1,0:T(8,128)(2,1)}, u32[]{:S(2)}) copy-start(bf16[512,2048]{1,0:T(8,128)(2,1)} %convolution_convert_fusion.1) | copy-start | bytes 6291460
  178.6 2.7 %collective-permute-start.6 = (bf16[256,2048]{1,0:T(8,128)(2,1)S(1)}, bf16[256,2048]{1,0:T(8,128)(2,1)S(1)}, u32[]{:S(2)}, u32[]{:S(2)}) collective-permute-start(bf16[256,2048]{1,0:T(8,128)(2,1)S(1)} %slice.65), channel_id=1, source_target_pairs={{0,1},{1,0},{2,3},{3,2},{4,5},{5,4},{6,7},{7,6},{8,9},{9,8},{10,11... | collective-permute-start | bytes 3145736 | tf_op jit(solution)/shard_map/ppermute | solution.py:96
  181.7 1.3 copy-start.2
  183.1 58.0 %collective-permute-start.7 = (bf16[128,2048]{1,0:T(8,128)(2,1)S(1)}, bf16[128,2048]{1,0:T(8,128)(2,1)}, u32[]{:S(2)}, u32[]{:S(2)}) collective-permute-start(bf16[128,2048]{1,0:T(8,128)(2,1)S(1)} %slice.128), channel_id=1, source_target_pairs={{0,2},{1,3},{2,0},{3,1},{4,6},{5,7},{6,4},{7,5},{8,10},{9,11},{10,... | collective-permute-start | bytes 1572872 | tf_op jit(solution)/shard_map/ppermute | solution.py:96
  237.4 2.0 copy-start.12
  237.4 2.4 copy-start.11
  240.2 1.6 copy-start.3
  240.2 1.7 copy-start.6

commit v2 on v1

--- a/solution.py
+++ b/solution.py
@@ -103,12 +103,15 @@
     return order
 
 
-def gather_lanes(values, lanes):
+def gather_lanes(values, lanes, beside=()):
     bit = lanes // 2
     while bit:
-        values = jnp.concatenate([values, lane_swap(values, bit, lanes)], axis=0)
+        arrived = lane_swap(values, bit, lanes)
+        if beside:
+            arrived, *beside = lax.optimization_barrier((arrived, *beside))
+        values = jnp.concatenate([values, arrived], axis=0)
         bit //= 2
-    return values
+    return (values, *beside)
 
 
 def sum_lanes(values, lanes):
@@ -121,16 +124,20 @@
     return total
 
 
-def attend(gathered, order, context_len, page_table, cache, gain, weight, bias, out_weight):
-    stretch, width = gathered.shape
-    lanes = weight.shape[2]
-    span = cache.shape[1] * cache.shape[2]
+def turn_tables(order, context_len):
     frequency = THETA ** (-(jnp.arange(HD // 2, dtype=jnp.float32) * 2.0 / HD))
     positions = context_len[0] + order
     angles = positions.astype(jnp.float32)[:, None] * frequency[None, :]
     cosines = jnp.tile(jnp.cos(angles), (1, 2))
     sines = jnp.sin(angles)
     sines = jnp.concatenate([-sines, sines], axis=1)
+    return cosines, sines
+
+
+def attend(gathered, order, cosines, sines, context_len, page_table, cache, gain, weight, bias, out_weight):
+    stretch, width = gathered.shape
+    lanes = weight.shape[2]
+    span = cache.shape[1] * cache.shape[2]
     smem = pl.BlockSpec(memory_space=pltpu.SMEM)
     vmem = pl.BlockSpec(memory_space=pltpu.VMEM)
     return pl.pallas_call(
@@ -205,11 +212,13 @@
     combine_high = combine.astype(jnp.bfloat16)
     combine_low = (combine - combine_high.astype(jnp.float32)).astype(jnp.bfloat16)
 
-    gathered = gather_lanes(hidden_in, head_lanes)
     owners = jnp.array(lane_order(head_lanes), jnp.int32) ^ lax.axis_index("head")
     order = (owners[:, None] * tok_rows + row_ids[None, :]).reshape(-1)
+    gathered, cosines, sines = gather_lanes(
+        hidden_in, head_lanes, turn_tables(order, context_len)
+    )
     attn_part = attend(
-        gathered, order, context_len, page_table, paged_cache, attn_gain, proj_weight, proj_bias, out_weight
+        gathered, order, cosines, sines, context_len, page_table, paged_cache, attn_gain, proj_weight, proj_bias, out_weight
     )
     attn_own = sum_lanes(attn_part, head_lanes)
     resid = (hidden_in.astype(jnp.float32) + attn_own).astype(jnp.bfloat16)
@@ -224,7 +233,7 @@
     sending = jnp.stack(buffer, axis=1).reshape(device_count, capacity, half)
     arrived = lax.all_to_all(sending, ("tok", "head"), split_axis=0, concat_axis=0, tiled=True)
 
-    mixed_all = gather_lanes(mixed, head_lanes)
+    mixed_all = gather_lanes(mixed, head_lanes)[0]
     inner = jnp.einsum("td,dcf->tcf", mixed_all, w_shared_in, preferred_element_type=jnp.float32)
     activated = (jax.nn.silu(inner[:, 0]) * inner[:, 1]).astype(jnp.bfloat16)
     shared_part = jnp.dot(activated, w_shared_out, preferred_element_type=jnp.float32).astype(

time: 245 us -> 245 us (level)
  local copies, waits for them, and re-layouts: 11.3 us -> 13.8 us
  transfers between devices with their start and end apart: 12 -> 12, of which waited for: 10 -> 11; matrix products, arithmetic and copies ran while one was open for 11% -> 11% of each run, Pallas kernels for 0% -> 0%
where the time goes in v2:
time: 245 us
  waiting for transfers between devices  132 us (54%)
  matrix products  34.2 us (14%)
  other arithmetic  23.9 us (10%)
  Pallas kernels  21 us (9%)
  starting transfers between devices  19.2 us (8%)
  local copies, waits for them, and re-layouts  13.8 us (6%)
    ppermute x8, waiting for transfers between devices, lane_swap(): lax.ppermute(values, 'head', [(lane, lane ^ bit) for lane in range(lanes)])  65.5 us
    all_to_all x1, waiting for transfers between devices, per_device(): lax.all_to_all(merged.reshape(device_count, capacity, half), ('tok', 'hea...  52.5 us
    pallas_call x1, Pallas kernels, attend(): pl.pallas_call(attend_kernel, out_shape=jax.ShapeDtypeStruct((stretch, wi...  21 us
    dot_general x1, matrix products, per_device(): inner = jnp.dot(tokens, w_experts_in[0], preferred_element_type=jnp.float32)  11.1 us
    dot_general x1, matrix products, per_device(): jnp.einsum('td,dcf->tcf', mixed_all, w_shared_in, preferred_element_type=...  10.6 us
    ppermute x8, starting transfers between devices, lane_swap(): lax.ppermute(values, 'head', [(lane, lane ^ bit) for lane in range(lanes)])  8.66 us
    all_to_all x1, starting transfers between devices, per_device(): lax.all_to_all(sending, ('tok', 'head'), split_axis=0, concat_axis=0, til...  6.37 us
    concatenate x3, other arithmetic, gather_lanes(): values = jnp.concatenate([values, arrived], axis=0)  5.49 us
  transfers between devices with their start and end apart: 12, of which 11 were waited for; matrix products, arithmetic and copies ran while one was open for 11% of the time, Pallas kernels for 0%

profile of v2, /device:TPU:0, one launch (start us, length us, event | category | flops | bytes accessed | tf_op | source)
XLA Modules:
  0.0 244.8 jit_solution(14959174903034212695)
XLA Ops:
  0.0 3.0 %collective-permute-start = (bf16[128,2048]{1,0:T(8,128)(2,1)}, bf16[128,2048]{1,0:T(8,128)(2,1)}, u32[]{:S(2)}, u32[]{:S(2)}) collective-permute-start(bf16[128,2048]{1,0:T(8,128)(2,1)} %param.17), channel_id=1, source_target_pairs={{0,2},{1,3},{2,0},{3,1},{4,6},{5,7},{6,4},{7,5},{8,10},{9,11},{10,... | collective-permute-start | bytes 1572872 | tf_op jit(solution)/shard_map/ppermute | solution.py:96
  3.7 0.7 xor_multiply_fusion
  4.4 1.8 fusion.35
  6.2 0.1 copy.36
  6.3 1.1 pad_maximum_fusion.4.sines
  7.4 7.9 %collective-permute-done = bf16[128,2048]{1,0:T(8,128)(2,1)} collective-permute-done((bf16[128,2048]{1,0:T(8,128)(2,1)}, bf16[128,2048]{1,0:T(8,128)(2,1)}, u32[]{:S(2)}, u32[]{:S(2)}) %collective-permute-start) | collective-permute-done | bytes 524320 | tf_op jit(solution)/shard_map/ppermute | solution.py:96
  15.3 0.7 tile.4
  16.0 2.3 pad_maximum_fusion.2
  18.3 0.1 copy.37.query_pos
  18.5 2.8 %collective-permute-done.1 = bf16[256,2048]{1,0:T(8,128)(2,1)} collective-permute-done((bf16[256,2048]{1,0:T(8,128)(2,1)}, bf16[256,2048]{1,0:T(8,128)(2,1)}, u32[]{:S(2)}, u32[]{:S(2)}) %collective-permute-start.1) | collective-permute-done | bytes 1048608 | tf_op jit(solution)/shard_map/ppermute | solution.py:96
  21.3 3.1 %pad_maximum_fusion.1.rows = bf16[512,2048]{1,0:T(8,128)(2,1)} fusion(bf16[256,2048]{1,0:T(8,128)(2,1)} %collective-permute-done.1, bf16[128,2048]{1,0:T(8,128)(2,1)} %collective-permute-done, bf16[128,2048]{1,0:T(8,128)(2,1)} %param.17), kind=kLoop, calls=%fused_computation.21 | loop fusion | flops 6291456 | bytes 4194304 | tf_op jit(solution)/shard_map/concatenate | solution.py:112
  24.4 1.8 copy.38.cosines
  26.2 0.9 copy-done.1
  27.1 21.0 %shard_map.163 = bf16[512,2048]{1,0:T(8,128)(2,1)} custom-call(s32[1,16]{1,0:T(1,128)S(1)} %copy-done.2, s32[1]{0:T(128)} %copy.47.context_len, bf16[512,2048]{1,0:T(8,128)(2,1)} %pad_maximum_fusion.1.rows, f32[1,2048]{1,0:T(1,128)S(1)} %bitcast.76, bf16[3,2048,512]{2,1,0:T(8,128)(2,1)} %weight.1, f32[3,1,512]{2,1,0:T(1,128)S(1)} %reshape.249.bias, ...), custom_call_target="tpu_custom_call" | custom-call | flops 12000000000 | bytes 20000000 | tf_op jit(solution)/shard_map/pallas_call | solution.py:143
  48.2 1.4 slice.75
  49.6 0.2 collective-permute-start.2
  49.9 2.5 %collective-permute-done.2 = bf16[256,2048]{1,0:T(8,128)(2,1)S(1)} collective-permute-done((bf16[256,2048]{1,0:T(8,128)(2,1)S(1)}, bf16[256,2048]{1,0:T(8,128)(2,1)S(1)}, u32[]{:S(2)}, u32[]{:S(2)}) %collective-permute-start.2) | collective-permute-done | bytes 1048608 | tf_op jit(solution)/shard_map/ppermute | solution.py:96
  52.4 0.4 convert_add_fusion.1
  52.7 1.4 copy-done.5
  54.1 0.9 slice.129
  54.9 1.7 collective-permute-start.3
  56.8 0.1 fusion.19
  56.9 0.2 bitcast_compare_fusion
  57.1 12.1 %collective-permute-done.3 = bf16[128,2048]{1,0:T(8,128)(2,1)} collective-permute-done((bf16[128,2048]{1,0:T(8,128)(2,1)}, bf16[128,2048]{1,0:T(8,128)(2,1)}, u32[]{:S(2)}, u32[]{:S(2)}) %collective-permute-start.3) | collective-permute-done | bytes 524320 | tf_op jit(solution)/shard_map/ppermute | solution.py:96
  69.3 1.7 fusion.24
  71.0 0.2 fusion.26
  71.2 0.6 copy-done.6
  71.8 0.5 convolution_convert_fusion.3
  72.3 0.5 convolution_convert_fusion.2
  72.8 1.8 pad_maximum_fusion
  74.5 6.4 %all-to-all-start = ((bf16[32,40,1024]{2,1,0:T(8,128)(2,1)}), bf16[32,40,1024]{2,1,0:T(8,128)(2,1)}, u32[]{:S(2)}, u32[]{:S(2)}) async-start(bf16[32,40,1024]{2,1,0:T(8,128)(2,1)} %bitcast.81), calls=%async_computation | async-start | bytes 5242880 | tf_op jit(solution)/shard_map/all_to_all | solution.py:234
  80.9 1.6 collective-permute-start.4
  82.5 36.8 %collective-permute-done.4 = bf16[128,2048]{1,0:T(8,128)(2,1)S(1)} collective-permute-done((bf16[128,2048]{1,0:T(8,128)(2,1)S(1)}, bf16[128,2048]{1,0:T(8,128)(2,1)S(1)}, u32[]{:S(2)}, u32[]{:S(2)}) %collective-permute-start.4) | collective-permute-done | bytes 524320 | tf_op jit(solution)/shard_map/ppermute | solution.py:96
  119.3 0.1 pad_maximum_fusion.3
  119.5 2.6 %collective-permute-done.5 = bf16[256,2048]{1,0:T(8,128)(2,1)S(1)} collective-permute-done((bf16[256,2048]{1,0:T(8,128)(2,1)S(1)}, bf16[256,2048]{1,0:T(8,128)(2,1)S(1)}, u32[]{:S(2)}, u32[]{:S(2)}) %collective-permute-start.5) | collective-permute-done | bytes 1048608 | tf_op jit(solution)/shard_map/ppermute | solution.py:96
  122.1 10.6 %fusion = f32[512,2,1408]{2,0,1:T(8,128)S(1)} fusion(bf16[2048,2,1408]{2,1,0:T(2,128)(2,1)} %param.30, bf16[256,2048]{1,0:T(8,128)(2,1)S(1)} %collective-permute-done.5, bf16[128,2048]{1,0:T(8,128)(2,1)S(1)} %collective-permute-done.4, bf16[128,2048]{1,0:T(8,128)(2,1)S(1)} %fusion.26), kind=kOutput, calls=%fused_computation | convolution fusion | flops 5911871488 | bytes 19398656 | tf_op jit(solution)/shard_map/td,dcf->tcf/dot_general | solution.py:237
  132.7 4.7 %convolution_convert_fusion.1 = bf16[512,2048]{1,0:T(8,128)(2,1)} fusion(bf16[1408,2048]{1,0:T(8,128)(2,1)S(1)} %bitcast.93, f32[512,2,1408]{2,0,1:T(8,128)S(1)} %fusion), kind=kOutput, calls=%fused_computation.11 | convolution fusion | flops 2958163968 | bytes 13631488 | tf_op jit(solution)/shard_map/dot_general | solution.py:239
  137.4 3.6 %all-to-all-done = bf16[32,40,1024]{2,1,0:T(8,128)(2,1)} async-done(((bf16[32,40,1024]{2,1,0:T(8,128)(2,1)}), bf16[32,40,1024]{2,1,0:T(8,128)(2,1)}, u32[]{:S(2)}, u32[]{:S(2)}) %all-to-all-start) | async-done | bytes 2621472 | tf_op jit(solution)/shard_map/all_to_all | solution.py:234
  141.1 5.2 %collective-permute-done.8 = bf16[1280,1024]{1,0:T(8,128)(2,1)} collective-permute-done((bf16[1280,1024]{1,0:T(8,128)(2,1)}, bf16[1280,1024]{1,0:T(8,128)(2,1)}, u32[]{:S(2)}, u32[]{:S(2)}) %collective-permute-start.8) | collective-permute-done | bytes 2621472 | tf_op jit(solution)/shard_map/ppermute | solution.py:247
  146.3 2.9 %broadcast_select_fusion.2 = (bf16[1280,1024]{1,0:T(8,128)(2,1)S(1)}, bf16[1280,1024]{1,0:T(8,128)(2,1)S(1)}) fusion(bf16[1280,1024]{1,0:T(8,128)(2,1)} %collective-permute-done.8, pred[]{:T(512)S(6)} %eq.79, bf16[32,40,1024]{2,1,0:T(8,128)(2,1)} %all-to-all-done), kind=kLoop, calls=%fused_computation.20 | loop fusion | flops 2621440 | bytes 10485761 | tf_op jit(solution)/shard_map/jit(_where)/select_n | solution.py:249
  149.2 11.1 %fusion.2 = f32[1280,1408]{1,0:T(8,128)S(1)} fusion(bf16[1,2048,1408]{2,1,0:T(8,128)(2,1)} %param.28, bf16[1280,1024]{1,0:T(8,128)(2,1)S(1)} %get-tuple-element.24, bf16[1280,1024]{1,0:T(8,128)(2,1)S(1)} %get-tuple-element.23), kind=kOutput, calls=%fused_computation.3 | convolution fusion | flops 7392460800 | bytes 18219008 | tf_op jit(solution)/shard_map/dot_general | solution.py:251
  160.3 4.9 %convolution_convert_fusion = bf16[1280,2048]{1,0:T(8,128)(2,1)S(1)} fusion(bf16[1,704,2048]{2,1,0:T(8,128)(2,1)S(1)} %copy-done, f32[1280,1408]{1,0:T(8,128)S(1)} %fusion.2), kind=kOutput, calls=%fused_computation.2 | convolution fusion | flops 3699015680 | bytes 15990784 | tf_op jit(solution)/shard_map/dot_general | solution.py:254
  165.2 0.3 broadcast_select_fusion
  165.5 0.2 collective-permute-start.9
  165.7 4.8 %collective-permute-done.9 = bf16[1280,1024]{1,0:T(8,128)(2,1)S(1)} collective-permute-done((bf16[1280,1024]{1,0:T(8,128)(2,1)S(1)}, bf16[1280,1024]{1,0:T(8,128)(2,1)S(1)}, u32[]{:S(2)}, u32[]{:S(2)}) %collective-permute-start.9) | collective-permute-done | bytes 2621472 | tf_op jit(solution)/shard_map/ppermute | solution.py:258
  170.4 3.5 %add_convert_fusion = bf16[1280,1024]{1,0:T(8,128)(2,1)} fusion(bf16[1280,1024]{1,0:T(8,128)(2,1)S(1)} %collective-permute-done.9, pred[]{:T(512)S(6)} %eq.79, bf16[1280,2048]{1,0:T(8,128)(2,1)S(1)} %convolution_convert_fusion), kind=kLoop, calls=%fused_computation.8 | loop fusion | flops 6553600 | bytes 10485761 | tf_op jit(solution)/shard_map/convert_element_type | solution.py:261
  173.9 3.9 %all-to-all-start.1 = ((bf16[32,40,1024]{2,1,0:T(8,128)(2,1)}), bf16[32,40,1024]{2,1,0:T(8,128)(2,1)}, u32[]{:S(2)}, u32[]{:S(2)}) async-start(bf16[32,40,1024]{2,1,0:T(8,128)(2,1)} %bitcast.82), calls=%async_computation.1 | async-start | bytes 5242880 | tf_op jit(solution)/shard_map/all_to_all | solution.py:262
  177.8 1.4 slice.65
  179.3 0.3 collective-permute-start.6
  179.6 0.7 select_convert_fusion
  180.3 0.7 fusion.32
  181.0 0.2 fusion.23
  181.2 0.8 collective-permute-done.6
  182.0 0.4 convert_add_fusion
  182.4 1.3 copy-done.3
  183.8 1.8 collective-permute-start.7
  185.5 52.5 %all-to-all-done.1 = bf16[32,40,1024]{2,1,0:T(8,128)(2,1)} async-done(((bf16[32,40,1024]{2,1,0:T(8,128)(2,1)}), bf16[32,40,1024]{2,1,0:T(8,128)(2,1)}, u32[]{:S(2)}, u32[]{:S(2)}) %all-to-all-start.1) | async-done | bytes 2621472 | tf_op jit(solution)/shard_map/all_to_all | solution.py:262
  238.1 2.0 fusion.42
  240.1 0.4 fusion.43
  240.5 0.4 convolution_add_fusion.1
  240.9 0.4 fusion.44
  241.3 0.4 convolution_add_fusion
  241.8 0.7 copy-done.4
  242.6 2.2 fusion.28
  (54 shorter events, 0.5 us)
Async XLA Ops:
  0.0 160.3 %copy-start = (bf16[1,704,2048]{2,1,0:T(8,128)(2,1)S(1)}, bf16[1,704,2048]{2,1,0:T(8,128)(2,1)}, u32[]{:S(2)}) copy-start(bf16[1,704,2048]{2,1,0:T(8,128)(2,1)} %param.29) | copy-start | bytes 8650756
  0.0 18.4 %copy-start.14 = (bf16[2048]{0:T(1024)(128)(2,1)S(1)}, bf16[2048]{0:T(1024)(128)(2,1)}, u32[]{:S(2)}) copy-start(bf16[2048]{0:T(1024)(128)(2,1)} %param.21) | copy-start | bytes 12292
  0.0 18.4 %copy-start.17 = (bf16[3,512]{1,0:T(4,128)(2,1)S(1)}, bf16[3,512]{1,0:T(4,128)(2,1)}, u32[]{:S(2)}) copy-start(bf16[3,512]{1,0:T(4,128)(2,1)} %param.23) | copy-start | bytes 9220
  0.0 15.2 %collective-permute-start = (bf16[128,2048]{1,0:T(8,128)(2,1)}, bf16[128,2048]{1,0:T(8,128)(2,1)}, u32[]{:S(2)}, u32[]{:S(2)}) collective-permute-start(bf16[128,2048]{1,0:T(8,128)(2,1)} %param.17), channel_id=1, source_target_pairs={{0,2},{1,3},{2,0},{3,1},{4,6},{5,7},{6,4},{7,5},{8,10},{9,11},{10,... | collective-permute-start | bytes 1572872 | tf_op jit(solution)/shard_map/ppermute | solution.py:96
  18.3 7.9 %copy-start.2 = (s32[1,16]{1,0:T(1,128)S(1)}, s32[1,16]{1,0:T(1,128)}, u32[]{:S(2)}) copy-start(s32[1,16]{1,0:T(1,128)} %table.1) | copy-start | bytes 196
  18.3 3.0 %collective-permute-start.1 = (bf16[256,2048]{1,0:T(8,128)(2,1)}, bf16[256,2048]{1,0:T(8,128)(2,1)}, u32[]{:S(2)}, u32[]{:S(2)}) collective-permute-start(bf16[256,2048]{1,0:T(8,128)(2,1)} %pad_maximum_fusion.2), channel_id=1, source_target_pairs={{0,1},{1,0},{2,3},{3,2},{4,5},{5,4},{6,7},{7,6},{8,9},{9,8},{10,11... | collective-permute-start | bytes 3145736 | tf_op jit(solution)/shard_map/ppermute | solution.py:96
  26.2 1.0 copy-start.1
  48.2 4.2 %copy-start.10 = (bf16[512,2048]{1,0:T(8,128)(2,1)S(1)}, bf16[512,2048]{1,0:T(8,128)(2,1)}, u32[]{:S(2)}) copy-start(bf16[512,2048]{1,0:T(8,128)(2,1)} %shard_map.163) | copy-start | bytes 6291460
  49.6 7.1 %copy-start.15 = (bf16[2048]{0:T(1024)(128)(2,1)S(1)}, bf16[2048]{0:T(1024)(128)(2,1)}, u32[]{:S(2)}) copy-start(bf16[2048]{0:T(1024)(128)(2,1)} %param.25) | copy-start | bytes 12292
  49.6 7.2 %copy-start.13 = (s32[128,4]{0,1:T(4,128)S(1)}, s32[128,4]{0,1:T(4,128)}, u32[]{:S(2)}) copy-start(s32[128,4]{0,1:T(4,128)} %param.26) | copy-start | bytes 6148
  49.6 19.6 %copy-start.8 = (bf16[128,2048]{1,0:T(8,128)(2,1)S(1)}, bf16[128,2048]{1,0:T(8,128)(2,1)}, u32[]{:S(2)}) copy-start(bf16[128,2048]{1,0:T(8,128)(2,1)} %param.17) | copy-start | bytes 1572868
  49.6 2.7 %collective-permute-start.2 = (bf16[256,2048]{1,0:T(8,128)(2,1)S(1)}, bf16[256,2048]{1,0:T(8,128)(2,1)S(1)}, u32[]{:S(2)}, u32[]{:S(2)}) collective-permute-start(bf16[256,2048]{1,0:T(8,128)(2,1)S(1)} %slice.75), channel_id=1, source_target_pairs={{0,1},{1,0},{2,3},{3,2},{4,5},{5,4},{6,7},{7,6},{8,9},{9,8},{10,11... | collective-permute-start | bytes 3145736 | tf_op jit(solution)/shard_map/ppermute | solution.py:96
  52.7 1.4 copy-start.5
  54.9 14.3 %collective-permute-start.3 = (bf16[128,2048]{1,0:T(8,128)(2,1)}, bf16[128,2048]{1,0:T(8,128)(2,1)}, u32[]{:S(2)}, u32[]{:S(2)}) collective-permute-start(bf16[128,2048]{1,0:T(8,128)(2,1)} %slice.129), channel_id=1, source_target_pairs={{0,2},{1,3},{2,0},{3,1},{4,6},{5,7},{6,4},{7,5},{8,10},{9,11},{10,... | collective-permute-start | bytes 1572872 | tf_op jit(solution)/shard_map/ppermute | solution.py:96
  71.0 0.8 copy-start.6
  74.5 66.5 %all-to-all-start = ((bf16[32,40,1024]{2,1,0:T(8,128)(2,1)}), bf16[32,40,1024]{2,1,0:T(8,128)(2,1)}, u32[]{:S(2)}, u32[]{:S(2)}) async-start(bf16[32,40,1024]{2,1,0:T(8,128)(2,1)} %bitcast.81), calls=%async_computation | async-start | bytes 5242880 | tf_op jit(solution)/shard_map/all_to_all | solution.py:234
  80.9 38.4 %collective-permute-start.4 = (bf16[128,2048]{1,0:T(8,128)(2,1)S(1)}, bf16[128,2048]{1,0:T(8,128)(2,1)S(1)}, u32[]{:S(2)}, u32[]{:S(2)}) collective-permute-start(bf16[128,2048]{1,0:T(8,128)(2,1)S(1)} %fusion.26), channel_id=1, source_target_pairs={{0,2},{1,3},{2,0},{3,1},{4,6},{5,7},{6,4},{7,5},{8,10},{9,11},{10,... | collective-permute-start | bytes 1572872 | tf_op jit(solution)/shard_map/ppermute | solution.py:96
  119.3 13.4 %slice-start = ((s8[5767168]{0:T(1024)(128)(4,1)}), s8[4194304]{0:T(1024)(128)(4,1)S(1)}, s32[]{:S(2)}) async-start(s8[5767168]{0:T(1024)(128)(4,1)} %bitcast.92), calls=%async_computation.2 | async-start | bytes 8388608
  119.4 13.3 %slice-start.1 = ((s8[5767168]{0:T(1024)(128)(4,1)}), s8[1572864]{0:T(1024)(128)(4,1)S(1)}, s32[]{:S(2)}) async-start(s8[5767168]{0:T(1024)(128)(4,1)} %bitcast.92), calls=%async_computation.3 | async-start | bytes 3145728
  119.4 2.7 %collective-permute-start.5 = (bf16[256,2048]{1,0:T(8,128)(2,1)S(1)}, bf16[256,2048]{1,0:T(8,128)(2,1)S(1)}, u32[]{:S(2)}, u32[]{:S(2)}) collective-permute-start(bf16[256,2048]{1,0:T(8,128)(2,1)S(1)} %pad_maximum_fusion.3), channel_id=1, source_target_pairs={{0,1},{1,0},{2,3},{3,2},{4,5},{5,4},{6,7},{7,6},{8,9},{9,8},{10,11... | collective-permute-start | bytes 3145736 | tf_op jit(solution)/shard_map/ppermute | solution.py:96
  141.1 5.3 %collective-permute-start.8 = (bf16[1280,1024]{1,0:T(8,128)(2,1)}, bf16[1280,1024]{1,0:T(8,128)(2,1)}, u32[]{:S(2)}, u32[]{:S(2)}) collective-permute-start(bf16[1280,1024]{1,0:T(8,128)(2,1)} %bitcast.19), channel_id=1, source_target_pairs={{0,1},{1,0},{2,3},{3,2},{4,5},{5,4},{6,7},{7,6},{8,9},{9,8},{10,11... | collective-permute-start | bytes 7864328 | tf_op jit(solution)/shard_map/ppermute | solution.py:247
  165.5 5.0 %collective-permute-start.9 = (bf16[1280,1024]{1,0:T(8,128)(2,1)S(1)}, bf16[1280,1024]{1,0:T(8,128)(2,1)S(1)}, u32[]{:S(2)}, u32[]{:S(2)}) collective-permute-start(bf16[1280,1024]{1,0:T(8,128)(2,1)S(1)} %broadcast_select_fusion), channel_id=1, source_target_pairs={{0,1},{1,0},{2,3},{3,2},{4,5},{5,4},{6,7},{7,6},{8,9},{9,8},{10,11... | collective-permute-start | bytes 7864328 | tf_op jit(solution)/shard_map/ppermute | solution.py:258
  173.9 5.6 %copy-start.16 = (bf16[2048]{0:T(1024)(128)(2,1)S(1)}, bf16[2048]{0:T(1024)(128)(2,1)}, u32[]{:S(2)}) copy-start(bf16[2048]{0:T(1024)(128)(2,1)} %param.32) | copy-start | bytes 12292
  173.9 5.7 %copy-start.18 = (f32[128,4]{0,1:T(4,128)S(1)}, f32[128,4]{0,1:T(4,128)}, u32[]{:S(2)}) copy-start(f32[128,4]{0,1:T(4,128)} %param.27) | copy-start | bytes 6148
  173.9 64.2 %all-to-all-start.1 = ((bf16[32,40,1024]{2,1,0:T(8,128)(2,1)}), bf16[32,40,1024]{2,1,0:T(8,128)(2,1)}, u32[]{:S(2)}, u32[]{:S(2)}) async-start(bf16[32,40,1024]{2,1,0:T(8,128)(2,1)} %bitcast.82), calls=%async_computation.1 | async-start | bytes 5242880 | tf_op jit(solution)/shard_map/all_to_all | solution.py:262
  177.8 4.2 %copy-start.9 = (bf16[512,2048]{1,0:T(8,128)(2,1)S(1)}, bf16[512,2048]{1,0:T(8,128)(2,1)}, u32[]{:S(2)}) copy-start(bf16[512,2048]{1,0:T(8,128)(2,1)} %convolution_convert_fusion.1) | copy-start | bytes 6291460
  179.3 2.7 %collective-permute-start.6 = (bf16[256,2048]{1,0:T(8,128)(2,1)S(1)}, bf16[256,2048]{1,0:T(8,128)(2,1)S(1)}, u32[]{:S(2)}, u32[]{:S(2)}) collective-permute-start(bf16[256,2048]{1,0:T(8,128)(2,1)S(1)} %slice.65), channel_id=1, source_target_pairs={{0,1},{1,0},{2,3},{3,2},{4,5},{5,4},{6,7},{7,6},{8,9},{9,8},{10,11... | collective-permute-start | bytes 3145736 | tf_op jit(solution)/shard_map/ppermute | solution.py:96
  182.4 1.3 copy-start.3
  183.8 58.0 %collective-permute-start.7 = (bf16[128,2048]{1,0:T(8,128)(2,1)S(1)}, bf16[128,2048]{1,0:T(8,128)(2,1)}, u32[]{:S(2)}, u32[]{:S(2)}) collective-permute-start(bf16[128,2048]{1,0:T(8,128)(2,1)S(1)} %slice.128), channel_id=1, source_target_pairs={{0,2},{1,3},{2,0},{3,1},{4,6},{5,7},{6,4},{7,5},{8,10},{9,11},{10,... | collective-permute-start | bytes 1572872 | tf_op jit(solution)/shard_map/ppermute | solution.py:96
  238.1 2.0 copy-start.12
  238.1 2.4 copy-start.11
  240.9 1.6 copy-start.4
  240.9 1.7 copy-start.7
